TPU v7x, 512 devices: a whole 4x8x8 slice. The times are simulated.
512 devices in a mesh: row: 32 (over y, x), layer: 16 (over z, core).
Axes of the slice: x: 4, y: 8, z: 8, core: 2. Of those that a mesh axis runs over, the one named last changes fastest.
Arguments:
- panel_left: bfloat16 [32, 32, 2048, 128], P('row', 'layer'), may hold values from -6 to 6
- panel_right: bfloat16 [32, 32, 2048, 128], P('row', 'layer'), may hold values from -0.125 to 0.125
- test_matrix: bfloat16 [2048, 128], replicated, may hold values from -6 to 6
- ranks: int32 [32, 32], P('row', 'layer'), may hold values from 32 to 128, as said below
- offsets: int32 [32, 2], P('row'), may hold values from 1 to 4, as said below
Outputs:
- basis: float32 [32, 2048, 2, 128], P('row', 'layer')
- update_right: float32 [32, 2048, 2, 128], P('row', 'layer')
Inputs may be any that keep to these rules, and one draw needn't show every extreme that they name: `ranks`: some tile has rank 128 and some tile has rank 128 // 4. An owner's 2 offsets differ from each other; the values 1 and 4 occur in every draw.
All inputs are finite; a program needn't handle non-finite values.
Results may differ from a plain program's by a relative error of at most 0.0003.
Values may be sent and summed in bfloat16 or wider, within the bound.
A program may use at most 64 MiB of HBM per device.

v0:
```python
import jax
import jax.numpy as jnp
from jax import lax
from jax.sharding import PartitionSpec as P

FRONTS = 4
TARGETS = 2


def passed_along(x, axis, by):
    length = lax.axis_size(axis)
    return lax.ppermute(x, axis, [(i, (i + by) % length) for i in range(length)])


def constant_of(front_item):
    return lambda: front_item


def orthonormal(sketch_rows, gram_mat):
    factor = jnp.linalg.cholesky(gram_mat)
    by_cols = jnp.transpose(sketch_rows, (1, 2, 0))
    solved = lax.linalg.triangular_solve(factor, by_cols, left_side=True, lower=True)
    return jnp.transpose(solved, (2, 0, 1))


def gram_of(sketch_rows, tile_size):
    return (
        jnp.einsum("bsr,bsq->srq", sketch_rows, sketch_rows, precision=lax.Precision.HIGHEST)
        / tile_size
    )


def on_device(panel_left, panel_right, test_matrix, ranks, offsets):
    high = lax.Precision.HIGHEST
    tile_size = panel_left.shape[2]
    rank_cap = panel_left.shape[3]
    share_rows = tile_size // lax.axis_size("layer")
    columns = lax.broadcasted_iota(jnp.int32, (ranks.shape[1], 1, rank_cap), 2)
    live_cols = (columns < ranks[0][:, None, None]).astype(jnp.bfloat16)
    own_left = panel_left[0] * live_cols
    own_right = panel_right[0] * live_cols
    stacked = jnp.stack([own_left, own_right])
    fronts = []
    moving = stacked
    for step_no in range(FRONTS):
        moving = passed_along(moving, "row", 1)
        fronts.append(moving)
    branches = [constant_of(front_item) for front_item in fronts]
    left_full = own_left.astype(jnp.float32)
    cores = []
    mixers = []
    partners = []
    for target in range(TARGETS):
        partner = lax.switch(offsets[0, target] - 1, branches)
        core_mat = jnp.einsum(
            "kbr,kbq->krq", own_right, partner[1], preferred_element_type=jnp.float32
        )
        probes = jnp.einsum(
            "kbr,bq->krq", partner[0], test_matrix, preferred_element_type=jnp.float32
        )
        mix_mat = jnp.einsum("krq,kqs->krs", core_mat, probes, precision=high)
        cores.append(core_mat)
        mixers.append(mix_mat)
        partners.append(partner[0].astype(jnp.float32))
    mixed = jnp.stack(mixers, axis=1)
    local_sketch = jnp.einsum("kbr,ksrq->bsq", left_full, mixed, precision=high)
    total_sketch = lax.psum(local_sketch, "layer")
    basis_all = orthonormal(total_sketch, gram_of(total_sketch, tile_size))
    first_own = lax.axis_index("layer") * share_rows
    basis_part = lax.dynamic_slice_in_dim(basis_all, first_own, share_rows, 0)
    reach = jnp.einsum("kbr,bsq->ksrq", left_full, basis_all, precision=high)
    weights = []
    for target in range(TARGETS):
        weight_mat = jnp.einsum("krq,krs->kqs", cores[target], reach[:, target], precision=high)
        weights.append(weight_mat)
    term_list = []
    for target in range(TARGETS):
        row_piece = lax.slice_in_dim(
            partners[target], 0, share_rows * lax.axis_size("layer"), axis=1
        )
        term_list.append(jnp.einsum("kbq,kqs->bs", row_piece, weights[target], precision=high))
    update_right = lax.psum_scatter(
        jnp.stack(term_list, axis=1) / tile_size, "layer", scatter_dimension=0, tiled=True
    )
    return (basis_part[None], update_right[None])


def solution(mesh):
    return jax.shard_map(
        on_device,
        mesh=mesh,
        in_specs=(
            P("row", "layer", None, None),
            P("row", "layer", None, None),
            P(),
            P("row", "layer"),
            P("row", None),
        ),
        out_specs=(P("row", "layer", None, None), P("row", "layer", None, None)),
        check_vma=False,
    )
```

profile of v0, /device:TPU:2, one launch (start us, length us, event | category | flops | bytes accessed | tf_op | source)
XLA Modules:
  0.0 479.9 jit_solution(14630520279900826652)
XLA Ops:
  8.0 1.7 broadcast_multiply_fusion.1
  9.9 3.4 collective-permute-start
  13.3 45.9 %collective-permute-done = bf16[2,2,2048,128]{3,2,1,0:T(8,128)(2,1)S(1)} collective-permute-done((bf16[2,2,2048,128]{3,2,1,0:T(8,128)(2,1)S(1)}, bf16[2,2,2048,128]{3,2,1,0:T(8,128)(2,1)S(1)}, u32[]{:S(2)}, u32[]{:S(2)}) %collective-permute-start) | collective-permute-done | bytes 2097184 | tf_op jit(solution)/shard_map/ppermute | solution.py:12
  59.2 3.4 collective-permute-start.1
  62.6 44.0 %collective-permute-done.1 = bf16[2,2,2048,128]{3,2,1,0:T(8,128)(2,1)S(1)} collective-permute-done((bf16[2,2,2048,128]{3,2,1,0:T(8,128)(2,1)S(1)}, bf16[2,2,2048,128]{3,2,1,0:T(8,128)(2,1)S(1)}, u32[]{:S(2)}, u32[]{:S(2)}) %collective-permute-start.1) | collective-permute-done | bytes 2097184 | tf_op jit(solution)/shard_map/ppermute | solution.py:12
  106.6 4.4 collective-permute-start.2
  110.9 43.6 %collective-permute-done.2 = bf16[2,2,2048,128]{3,2,1,0:T(8,128)(2,1)} collective-permute-done((bf16[2,2,2048,128]{3,2,1,0:T(8,128)(2,1)S(1)}, bf16[2,2,2048,128]{3,2,1,0:T(8,128)(2,1)}, u32[]{:S(2)}, u32[]{:S(2)}) %collective-permute-start.2) | collective-permute-done | bytes 2097184 | tf_op jit(solution)/shard_map/ppermute | solution.py:12
  154.5 4.0 collective-permute-start.3
  160.4 41.0 %collective-permute-done.3 = bf16[2,2,2048,128]{3,2,1,0:T(8,128)(2,1)} collective-permute-done((bf16[2,2,2048,128]{3,2,1,0:T(8,128)(2,1)}, bf16[2,2,2048,128]{3,2,1,0:T(8,128)(2,1)}, u32[]{:S(2)}, u32[]{:S(2)}) %collective-permute-start.3) | collective-permute-done | bytes 2097184 | tf_op jit(solution)/shard_map/ppermute | solution.py:12
  201.4 3.1 conditional.2
  201.4 3.1 copy.36
  204.5 2.0 fusion.8
  206.5 2.2 fusion.7
  210.4 2.3 convolution_bitcast_fusion
  213.0 138.5 %all-reduce.2.cloned.1.call-done = f32[2048,2,128]{2,0,1:T(8,128)} async-done(((f32[2048,2,128]{2,0,1:T(8,128)}), f32[2048,2,128]{2,0,1:T(8,128)}) %all-reduce.2.cloned.1.call-update) | async-done | bytes 2097168 | tf_op jit(solution)/shard_map/psum | solution.py:67
  351.6 5.8 %fusion.28 = f32[2,128,128]{2,1,0:T(8,128)S(1)} fusion(f32[2048,2,128]{2,0,1:T(8,128)} %all-reduce.2.cloned.1.call-done), kind=kOutput, calls=%fused_computation.51 | convolution fusion | flops 805306368 | bytes 2228224 | tf_op jit(solution)/shard_map/bsr,bsq->srq/dot_general | solution.py:28
  357.5 23.5 %custom-call.7 = f32[2,128,128]{2,1,0:T(8,128)S(1)} custom-call(f32[2,128,128]{2,1,0:T(8,128)S(1)} %fusion.25), custom_call_target="Cholesky" | custom-call | tf_op jit(solution)/shard_map/jit(cholesky)/cholesky | solution.py:20
  381.2 19.9 %custom-call.8 = f32[2,1,128,128]{2,3,1,0:T(8,128)S(1)} custom-call(f32[2,1,128,128]{3,2,1,0:T(8,128)S(1)} %select_bitcast_fusion), custom_call_target="InvertDiagBlocksLowerTriangular" | custom-call | tf_op jit(solution)/shard_map/triangular_solve | solution.py:22
  401.2 2.0 fusion.2
  403.1 1.2 fusion.4
  406.5 1.0 convolution_bitcast_fusion.2
  407.5 1.4 maximum_multiply_fusion
  410.7 60.7 %reduce-scatter.2.cloned.1.call-done = f32[128,2,128]{2,0,1:T(8,128)} async-done(((f32[2048,2,128]{2,0,1:T(8,128)}), f32[128,2,128]{2,0,1:T(8,128)}) %reduce-scatter.2.cloned.1.call-update) | async-done | bytes 131088 | tf_op jit(solution)/shard_map/reduce_scatter | solution.py:82
  471.4 1.7 copy.22
  (46 shorter events, 7.7 us)
Async XLA Ops:
  7.2 201.6 %copy-start = (bf16[2048,128]{1,0:T(8,128)(2,1)S(1)}, bf16[2048,128]{1,0:T(8,128)(2,1)}, u32[]{:S(2)}) copy-start(bf16[2048,128]{1,0:T(8,128)(2,1)} %param.15) | copy-start | bytes 1572868
  7.2 344.4 %all-reduce.2.cloned.1.call-start = ((), (), s32[]{:S(2)}) async-start(), calls=%async_computation.1 | async-start | bytes 4194304 | tf_op jit(solution)/shard_map/psum | solution.py:67
  9.7 148.8 %copy-start.10 = (s32[1,2]{1,0:T(1,128)S(1)}, s32[1,2]{1,0:T(1,128)}, u32[]{:S(2)}) copy-start(s32[1,2]{1,0:T(1,128)} %param.17) | copy-start | bytes 28
  9.9 49.3 %collective-permute-start = (bf16[2,2,2048,128]{3,2,1,0:T(8,128)(2,1)S(1)}, bf16[2,2,2048,128]{3,2,1,0:T(8,128)(2,1)S(1)}, u32[]{:S(2)}, u32[]{:S(2)}) collective-permute-start(bf16[2,2,2048,128]{3,2,1,0:T(8,128)(2,1)S(1)} %pad_maximum_fusion), channel_id=1, source_target_pairs={{0,16},{16,32},{32,48},{48,64},{64,80},{80,96},{96,112},{112,128},... | collective-permute-start | bytes 6291464 | tf_op jit(solution)/shard_map/ppermute | solution.py:12
  59.2 142.2 %copy-start.5 = (bf16[2,2,2048,128]{3,2,1,0:T(8,128)(2,1)}, bf16[2,2,2048,128]{3,2,1,0:T(8,128)(2,1)S(1)}, u32[]{:S(2)}) copy-start(bf16[2,2,2048,128]{3,2,1,0:T(8,128)(2,1)S(1)} %collective-permute-done) | copy-start | bytes 6291460
  59.2 47.4 %collective-permute-start.1 = (bf16[2,2,2048,128]{3,2,1,0:T(8,128)(2,1)S(1)}, bf16[2,2,2048,128]{3,2,1,0:T(8,128)(2,1)S(1)}, u32[]{:S(2)}, u32[]{:S(2)}) collective-permute-start(bf16[2,2,2048,128]{3,2,1,0:T(8,128)(2,1)S(1)} %collective-permute-done), channel_id=1, source_target_pairs={{0,16},{16,32},{32,48},{48,64},{64,80},{80,96},{96,112},{112,128},... | collective-permute-start | bytes 6291464 | tf_op jit(solution)/shard_map/ppermute | solution.py:12
  106.6 48.0 %collective-permute-start.2 = (bf16[2,2,2048,128]{3,2,1,0:T(8,128)(2,1)S(1)}, bf16[2,2,2048,128]{3,2,1,0:T(8,128)(2,1)}, u32[]{:S(2)}, u32[]{:S(2)}) collective-permute-start(bf16[2,2,2048,128]{3,2,1,0:T(8,128)(2,1)S(1)} %collective-permute-done.1), channel_id=1, source_target_pairs={{0,16},{16,32},{32,48},{48,64},{64,80},{80,96},{96,112},{112,128},... | collective-permute-start | bytes 6291464 | tf_op jit(solution)/shard_map/ppermute | solution.py:12
  154.5 46.9 %collective-permute-start.3 = (bf16[2,2,2048,128]{3,2,1,0:T(8,128)(2,1)}, bf16[2,2,2048,128]{3,2,1,0:T(8,128)(2,1)}, u32[]{:S(2)}, u32[]{:S(2)}) collective-permute-start(bf16[2,2,2048,128]{3,2,1,0:T(8,128)(2,1)} %collective-permute-done.2), channel_id=1, source_target_pairs={{0,16},{16,32},{32,48},{48,64},{64,80},{80,96},{96,112},{112,128},... | collective-permute-start | bytes 6291464 | tf_op jit(solution)/shard_map/ppermute | solution.py:12
  206.5 2.2 copy-start.8
  206.5 2.8 copy-start.6
  208.7 1.7 copy-start.2
  212.8 258.6 %reduce-scatter.2.cloned.1.call-start = ((), (), s32[]{:S(2)}) async-start(), calls=%async_computation.2 | async-start | bytes 2228224 | tf_op jit(solution)/shard_map/reduce_scatter | solution.py:82
  351.6 49.6 %copy-start.1 = (f32[2048,2,128]{2,0,1:T(8,128)S(1)}, f32[2048,2,128]{2,0,1:T(8,128)}, u32[]{:S(2)}) copy-start(f32[2048,2,128]{2,0,1:T(8,128)} %all-reduce.2.cloned.1.call-done) | copy-start | bytes 6291460
  401.1 2.0 copy-start.3
  403.1 2.0 copy-start.4
  403.1 2.3 copy-start.7
  404.3 2.2 copy-start.9
Sparse Core Ops, SparseCore 0:
  212.9 138.6 all-reduce.1
  409.1 62.2 reduce-scatter.1
where the time goes:
time: 480 us
  waiting for transfers between devices  374 us (78%)
  other arithmetic  47.7 us (10%)
  matrix products  19.8 us (4%)
  between operations  15.7 us (3%)
  starting transfers between devices  15.4 us (3%)
  local copies, waits for them, and re-layouts  7.61 us (2%)
    ppermute x4, waiting for transfers between devices, passed_along(): lax.ppermute(x, axis, [(i, (i + by) % length) for i in range(length)])  174 us
    psum x1, waiting for transfers between devices, on_device(): total_sketch = lax.psum(local_sketch, 'layer')  139 us
    reduce_scatter x1, waiting for transfers between devices, on_device(): lax.psum_scatter(jnp.stack(term_list, axis=1) / tile_size, 'layer', scatt...  60.7 us
    another operation x4, other arithmetic, orthonormal(): factor = jnp.linalg.cholesky(gram_mat)  23.6 us
    another operation x3, other arithmetic, orthonormal(): lax.linalg.triangular_solve(factor, by_cols, left_side=True, lower=True)  20 us
    ppermute x4, starting transfers between devices, passed_along(): lax.ppermute(x, axis, [(i, (i + by) % length) for i in range(length)])  15.1 us
  transfers between devices with their start and end apart: 6, of which 6 were waited for; matrix products, arithmetic and copies ran while one was open for 0% of the time, Pallas kernels for 0%

commit v1 on v0

--- a/solution.py
+++ b/solution.py
@@ -64,7 +64,8 @@
         partners.append(partner[0].astype(jnp.float32))
     mixed = jnp.stack(mixers, axis=1)
     local_sketch = jnp.einsum("kbr,ksrq->bsq", left_full, mixed, precision=high)
-    total_sketch = lax.psum(local_sketch, "layer")
+    blocks = lax.all_gather(local_sketch, "layer", axis=0, tiled=False)
+    total_sketch = blocks.sum(axis=0)
     basis_all = orthonormal(total_sketch, gram_of(total_sketch, tile_size))
     first_own = lax.axis_index("layer") * share_rows
     basis_part = lax.dynamic_slice_in_dim(basis_all, first_own, share_rows, 0)

time: 480 us -> 546 us (1.14)
  waiting for transfers between devices: 374 us -> 429 us
  other arithmetic: 47.7 us -> 59.5 us
    all_gather x0 -> x1, waiting for transfers between devices: none -> 195 us  [on_device(): blocks = lax.all_gather(local_sketch, 'layer', axis=0, tiled=False)]
    psum x1 -> x0, waiting for transfers between devices: 139 us -> none  [on_device(): total_sketch = lax.psum(local_sketch, 'layer')]
    reduce_sum x0 -> x1, other arithmetic: none -> 11.8 us  [on_device(): total_sketch = blocks.sum(axis=0)]
where the time goes in v1:
time: 546 us; the launch traced here: 545 us
  waiting for transfers between devices  429 us (79%)
  other arithmetic  59.5 us (11%)
  matrix products  18.8 us (3%)
  between operations  15.6 us (3%)
  starting transfers between devices  15.4 us (3%)
  local copies, waits for them, and re-layouts  7.45 us (1%)
    all_gather x1, waiting for transfers between devices, on_device(): blocks = lax.all_gather(local_sketch, 'layer', axis=0, tiled=False)  195 us
    ppermute x4, waiting for transfers between devices, passed_along(): lax.ppermute(x, axis, [(i, (i + by) % length) for i in range(length)])  174 us
    reduce_scatter x1, waiting for transfers between devices, on_device(): lax.psum_scatter(jnp.stack(term_list, axis=1) / tile_size, 'layer', scatt...  59.2 us
    another operation x4, other arithmetic, orthonormal(): factor = jnp.linalg.cholesky(gram_mat)  23.6 us
    another operation x3, other arithmetic, orthonormal(): lax.linalg.triangular_solve(factor, by_cols, left_side=True, lower=True)  20 us
    ppermute x4, starting transfers between devices, passed_along(): lax.ppermute(x, axis, [(i, (i + by) % length) for i in range(length)])  15.1 us
    reduce_sum x1, other arithmetic, on_device(): total_sketch = blocks.sum(axis=0)  11.8 us
  transfers between devices with their start and end apart: 6, of which 6 were waited for; matrix products, arithmetic and copies ran while one was open for 0% of the time, Pallas kernels for 0%

profile of v1, /device:TPU:2, one launch (start us, length us, event | category | flops | bytes accessed | tf_op | source)
XLA Modules:
  0.0 545.5 jit_solution(13776478301894709389)
XLA Ops:
  8.0 1.7 broadcast_multiply_fusion.1
  9.9 3.4 collective-permute-start
  13.3 45.9 %collective-permute-done = bf16[2,2,2048,128]{3,2,1,0:T(8,128)(2,1)S(1)} collective-permute-done((bf16[2,2,2048,128]{3,2,1,0:T(8,128)(2,1)S(1)}, bf16[2,2,2048,128]{3,2,1,0:T(8,128)(2,1)S(1)}, u32[]{:S(2)}, u32[]{:S(2)}) %collective-permute-start) | collective-permute-done | bytes 2097184 | tf_op jit(solution)/shard_map/ppermute | solution.py:12
  59.2 3.4 collective-permute-start.1
  62.6 44.0 %collective-permute-done.1 = bf16[2,2,2048,128]{3,2,1,0:T(8,128)(2,1)S(1)} collective-permute-done((bf16[2,2,2048,128]{3,2,1,0:T(8,128)(2,1)S(1)}, bf16[2,2,2048,128]{3,2,1,0:T(8,128)(2,1)S(1)}, u32[]{:S(2)}, u32[]{:S(2)}) %collective-permute-start.1) | collective-permute-done | bytes 2097184 | tf_op jit(solution)/shard_map/ppermute | solution.py:12
  106.6 4.4 collective-permute-start.2
  110.9 43.6 %collective-permute-done.2 = bf16[2,2,2048,128]{3,2,1,0:T(8,128)(2,1)} collective-permute-done((bf16[2,2,2048,128]{3,2,1,0:T(8,128)(2,1)S(1)}, bf16[2,2,2048,128]{3,2,1,0:T(8,128)(2,1)}, u32[]{:S(2)}, u32[]{:S(2)}) %collective-permute-start.2) | collective-permute-done | bytes 2097184 | tf_op jit(solution)/shard_map/ppermute | solution.py:12
  154.5 4.0 collective-permute-start.3
  160.4 41.0 %collective-permute-done.3 = bf16[2,2,2048,128]{3,2,1,0:T(8,128)(2,1)} collective-permute-done((bf16[2,2,2048,128]{3,2,1,0:T(8,128)(2,1)}, bf16[2,2,2048,128]{3,2,1,0:T(8,128)(2,1)}, u32[]{:S(2)}, u32[]{:S(2)}) %collective-permute-start.3) | collective-permute-done | bytes 2097184 | tf_op jit(solution)/shard_map/ppermute | solution.py:12
  201.4 3.0 conditional.2
  201.4 3.0 copy.59
  204.4 2.2 fusion.8
  207.2 2.1 fusion.7
  209.3 1.7 fusion.12
  211.5 2.4 convolution_bitcast_fusion
  214.2 195.1 %all-gather.3.cloned.1.call-done = f32[32768,2,128]{2,0,1:T(8,128)} async-done(((f32[2048,2,128]{2,0,1:T(8,128)}), f32[32768,2,128]{2,0,1:T(8,128)}) %all-gather.3.cloned.1.call-update) | async-done | bytes 33554448 | tf_op jit(solution)/shard_map/all_gather | solution.py:67
  409.3 11.8 %reduce_sum.9 = f32[2048,2,128]{2,0,1:T(8,128)S(1)} reduce(f32[16,2048,2,128]{3,1,0,2:T(8,128)} %bitcast.101, f32[]{:T(128)} %constant.64.clone.1), dimensions={0}, to_apply=%region_8.0 | reduce | flops 7864320 | bytes 35651588 | tf_op jit(solution)/shard_map/reduce_sum | solution.py:68
  421.1 3.5 fusion.28
  424.7 23.5 %custom-call.7 = f32[2,128,128]{2,1,0:T(8,128)S(1)} custom-call(f32[2,128,128]{2,1,0:T(8,128)S(1)} %fusion.25), custom_call_target="Cholesky" | custom-call | tf_op jit(solution)/shard_map/jit(cholesky)/cholesky | solution.py:20
  448.4 19.9 %custom-call.8 = f32[2,1,128,128]{2,3,1,0:T(8,128)S(1)} custom-call(f32[2,1,128,128]{3,2,1,0:T(8,128)S(1)} %select_bitcast_fusion), custom_call_target="InvertDiagBlocksLowerTriangular" | custom-call | tf_op jit(solution)/shard_map/triangular_solve | solution.py:22
  468.3 2.0 fusion.2
  474.6 1.5 maximum_multiply_fusion
  477.8 59.2 %reduce-scatter.2.cloned.1.call-done = f32[128,2,128]{2,0,1:T(8,128)} async-done(((f32[2048,2,128]{2,0,1:T(8,128)}), f32[128,2,128]{2,0,1:T(8,128)}) %reduce-scatter.2.cloned.1.call-update) | async-done | bytes 131088 | tf_op jit(solution)/shard_map/reduce_scatter | solution.py:83
  537.0 1.7 copy.37
  (43 shorter events, 9.3 us)
Async XLA Ops:
  7.2 199.4 %copy-start = (bf16[2048,128]{1,0:T(8,128)(2,1)S(1)}, bf16[2048,128]{1,0:T(8,128)(2,1)}, u32[]{:S(2)}) copy-start(bf16[2048,128]{1,0:T(8,128)(2,1)} %param.15) | copy-start | bytes 1572868
  7.2 402.1 %all-gather.3.cloned.1.call-start = ((), (), s32[]{:S(2)}) async-start(), calls=%async_computation.2 | async-start | bytes 35651584 | tf_op jit(solution)/shard_map/all_gather | solution.py:67
  9.7 148.8 %copy-start.8 = (s32[1,2]{1,0:T(1,128)S(1)}, s32[1,2]{1,0:T(1,128)}, u32[]{:S(2)}) copy-start(s32[1,2]{1,0:T(1,128)} %param.17) | copy-start | bytes 28
  9.9 49.3 %collective-permute-start = (bf16[2,2,2048,128]{3,2,1,0:T(8,128)(2,1)S(1)}, bf16[2,2,2048,128]{3,2,1,0:T(8,128)(2,1)S(1)}, u32[]{:S(2)}, u32[]{:S(2)}) collective-permute-start(bf16[2,2,2048,128]{3,2,1,0:T(8,128)(2,1)S(1)} %pad_maximum_fusion), channel_id=1, source_target_pairs={{0,16},{16,32},{32,48},{48,64},{64,80},{80,96},{96,112},{112,128},... | collective-permute-start | bytes 6291464 | tf_op jit(solution)/shard_map/ppermute | solution.py:12
  59.2 142.2 %copy-start.4 = (bf16[2,2,2048,128]{3,2,1,0:T(8,128)(2,1)}, bf16[2,2,2048,128]{3,2,1,0:T(8,128)(2,1)S(1)}, u32[]{:S(2)}) copy-start(bf16[2,2,2048,128]{3,2,1,0:T(8,128)(2,1)S(1)} %collective-permute-done) | copy-start | bytes 6291460
  59.2 47.4 %collective-permute-start.1 = (bf16[2,2,2048,128]{3,2,1,0:T(8,128)(2,1)S(1)}, bf16[2,2,2048,128]{3,2,1,0:T(8,128)(2,1)S(1)}, u32[]{:S(2)}, u32[]{:S(2)}) collective-permute-start(bf16[2,2,2048,128]{3,2,1,0:T(8,128)(2,1)S(1)} %collective-permute-done), channel_id=1, source_target_pairs={{0,16},{16,32},{32,48},{48,64},{64,80},{80,96},{96,112},{112,128},... | collective-permute-start | bytes 6291464 | tf_op jit(solution)/shard_map/ppermute | solution.py:12
  106.6 48.0 %collective-permute-start.2 = (bf16[2,2,2048,128]{3,2,1,0:T(8,128)(2,1)S(1)}, bf16[2,2,2048,128]{3,2,1,0:T(8,128)(2,1)}, u32[]{:S(2)}, u32[]{:S(2)}) collective-permute-start(bf16[2,2,2048,128]{3,2,1,0:T(8,128)(2,1)S(1)} %collective-permute-done.1), channel_id=1, source_target_pairs={{0,16},{16,32},{32,48},{48,64},{64,80},{80,96},{96,112},{112,128},... | collective-permute-start | bytes 6291464 | tf_op jit(solution)/shard_map/ppermute | solution.py:12
  154.5 46.9 %collective-permute-start.3 = (bf16[2,2,2048,128]{3,2,1,0:T(8,128)(2,1)}, bf16[2,2,2048,128]{3,2,1,0:T(8,128)(2,1)}, u32[]{:S(2)}, u32[]{:S(2)}) collective-permute-start(bf16[2,2,2048,128]{3,2,1,0:T(8,128)(2,1)} %collective-permute-done.2), channel_id=1, source_target_pairs={{0,16},{16,32},{32,48},{48,64},{64,80},{80,96},{96,112},{112,128},... | collective-permute-start | bytes 6291464 | tf_op jit(solution)/shard_map/ppermute | solution.py:12
  204.4 2.2 copy-start.6
  207.2 4.4 copy-start.1
  214.0 323.0 %reduce-scatter.2.cloned.1.call-start = ((), (), s32[]{:S(2)}) async-start(), calls=%async_computation.1 | async-start | bytes 2228224 | tf_op jit(solution)/shard_map/reduce_scatter | solution.py:83
  468.3 2.0 copy-start.2
  470.3 2.0 copy-start.3
  470.3 2.3 copy-start.7
  471.5 2.2 copy-start.5
Sparse Core Ops, SparseCore 0:
  214.1 195.1 all-gather.2
  476.3 60.6 reduce-scatter.1
